TPU v7x, 32 devices: a whole 2x2x4 slice. The times are simulated.
32 devices in a mesh: groups: 2 (over y), inst: 4 (over z), tp: 4 (over x, core).
Axes of the slice: x: 2, y: 2, z: 4, core: 2. Of those that a mesh axis runs over, the one named last changes fastest.
Arguments:
- hidden: bfloat16 [2, 1024, 8192], P(None, ('groups', 'inst'), 'tp'), parts along dimension 1, may hold values from -6 to 6
- key_matrix: bfloat16 [8192, 1024], P('tp'), may hold values from -0.0625 to 0.0625
- adapter_down_weight: bfloat16 [256, 16, 8192], P('inst', None, 'tp'), may hold values from -0.0625 to 0.0625
- adapter_up_weight: bfloat16 [256, 16, 1024], P('inst', None, 'tp'), may hold values from -1.5 to 1.5
- request_adapter_slot: int32 [1024], P(('groups', 'inst')), parts along dimension 0, may hold values from 0 to 31, as said below
- adapter_pool_rows: int32 [64], P('groups'), parts along dimension 0, may hold values from 0 to 255, as said below
- lengths: int32 [1024], P(('groups', 'inst')), parts along dimension 0, may hold values from 1 to 4095
Outputs:
- new_keys: bfloat16 [2, 1024, 1024], P(None, ('groups', 'inst'), 'tp'), parts along dimension 1
There are 2 independent parts, one for each index of `groups`. A program takes and returns all parts, laid end to end along the dimension named above; an argument that names none is the same for every part. Nothing has to cross between parts.
Inputs may be any that keep to these rules, and one draw needn't show every extreme that they name: `adapter_pool_rows`: adapter in use k lies in the pool rows of instance j = k // 8, that is rows j * 64 to j * 64 + 63; the rows of the pool are held in order by the instances, 64 each; the 32 rows are distinct. `request_adapter_slot`: at most 64 of the 128 requests of one instance use adapters held by one instance, and one instance, the same for all, receives exactly 64 from every instance.
All inputs are finite; a program needn't handle non-finite values.
Results may differ from a plain program's by a relative error of at most 0.0055.
Values may be sent and summed in bfloat16 or wider, within the bound.
A program may use at most 64 MiB of HBM per device.

v0:
```python
import jax
import jax.numpy as jnp
from jax import lax
from jax.sharding import PartitionSpec as P

HEAD = 128


adapter_scale = 2.0
rope_theta = 500000.0


def rope_freqs(head_size):
    pair_index = jnp.arange(head_size // 2, dtype=jnp.float32)
    base_freq = rope_theta ** (-2.0 * pair_index / head_size)
    wavelen = 2.0 * jnp.pi / base_freq
    smooth = (8192.0 / wavelen - 1.0) / 3.0
    blended = (1.0 - smooth) * base_freq / 8.0 + smooth * base_freq
    scaled = jnp.where(wavelen > 8192.0, base_freq / 8.0, blended)
    return jnp.where(wavelen < 2048.0, base_freq, scaled)


def apply_rope(values, positions, head_size):
    row_count = values.shape[0]
    head_count = values.shape[1] // head_size
    shaped = values.reshape(row_count, head_count, head_size)
    angles = positions.astype(jnp.float32)[:, None] * rope_freqs(head_size)[None, :]
    cosine = jnp.cos(angles)[:, None, :]
    sine_part = jnp.sin(angles)[:, None, :]
    half_head = head_size // 2
    first_half = shaped[:, :, :half_head]
    second = shaped[:, :, half_head:]
    turned = jnp.concatenate(
        [first_half * cosine - second * sine_part, second * cosine + first_half * sine_part], axis=2
    )
    return turned.reshape(row_count, head_count * head_size)


def on_device(
    hidden,
    key_matrix,
    adapter_down_weight,
    adapter_up_weight,
    request_adapter_slot,
    adapter_pool_rows,
    lengths,
):
    num_steps, requests, feature_width = hidden.shape
    inst_count = lax.axis_size("inst")
    active_count = adapter_pool_rows.shape[0] // inst_count
    pool_row_count = adapter_down_weight.shape[0]
    adapter_rank_width = adapter_down_weight.shape[1]
    key_local_part = adapter_up_weight.shape[2]
    own_index = lax.axis_index("inst")
    flat_rows = hidden.reshape(num_steps * requests, feature_width)
    partial_keys = jnp.dot(flat_rows, key_matrix, preferred_element_type=jnp.float32)
    plain_keys = lax.psum_scatter(partial_keys, "tp", scatter_dimension=1, tiled=True)
    request_pool_rows = (
        lax.dynamic_slice_in_dim(adapter_pool_rows, own_index * active_count, active_count)
        - own_index * pool_row_count
    )
    request_down_weight = jnp.take(adapter_down_weight, request_pool_rows, axis=0)
    request_up_weight = jnp.take(adapter_up_weight, request_pool_rows, axis=0)
    row_slot = jnp.tile(request_adapter_slot, num_steps)
    shard_piece = (
        lax.all_gather(request_down_weight, "inst", axis=0, tiled=True),
        lax.all_gather(request_up_weight, "inst", axis=0, tiled=True),
    )
    piece_count = shard_piece[0].shape[0]
    down_piece = shard_piece[0].reshape(piece_count * adapter_rank_width, feature_width)
    scores = lax.dot_general(
        flat_rows, down_piece, (((1,), (1,)), ((), ())), preferred_element_type=jnp.float32
    )
    slot_hits = row_slot[:, None] == jnp.arange(piece_count, dtype=jnp.int32)[None, :]
    chosen = jnp.sum(
        scores.reshape(-1, piece_count, adapter_rank_width)
        * slot_hits[:, :, None].astype(jnp.float32),
        axis=1,
    )
    up_rows = jnp.dot(
        slot_hits.astype(jnp.bfloat16),
        shard_piece[1].reshape(piece_count, adapter_rank_width * key_local_part),
        preferred_element_type=jnp.float32,
    )
    picked_up = up_rows.astype(jnp.bfloat16)
    shrink = lax.psum(chosen, "tp").astype(jnp.bfloat16)
    update_rows = jnp.einsum(
        "rk,rkc->rc",
        shrink,
        picked_up.reshape(-1, adapter_rank_width, key_local_part),
        preferred_element_type=jnp.float32,
    ).astype(jnp.bfloat16)
    combined_keys = plain_keys + adapter_scale * update_rows.astype(jnp.float32)
    positions = jnp.concatenate([lengths + step_index for step_index in range(num_steps)])
    turned = apply_rope(combined_keys, positions, HEAD)
    return turned.astype(jnp.bfloat16).reshape(num_steps, requests, key_local_part)


def solution(mesh):
    placed = (
        P(None, ("groups", "inst"), "tp"),
        P("tp", None),
        P("inst", None, "tp"),
        P("inst", None, "tp"),
        P(("groups", "inst")),
        P("groups"),
        P(("groups", "inst")),
    )
    return jax.shard_map(
        on_device,
        mesh=mesh,
        in_specs=placed,
        out_specs=P(None, ("groups", "inst"), "tp"),
        check_vma=False,
    )
```

profile of v0, /device:TPU:0, one launch (start us, length us, event | category | flops | bytes accessed | tf_op | source)
XLA Modules:
  0.0 89.0 jit_solution(14277622441733129608)
XLA Ops:
  7.4 0.8 compare_and_fusion
  8.2 2.8 %gather_fusion = bf16[8,16,2048]{2,1,0:T(8,128)(2,1)S(1)} fusion(bf16[64,16,2048]{2,1,0:T(8,128)(2,1)} %param.9, s32[1024]{0:T(1024)S(1)} %pad_clamp_fusion), kind=kCustom, calls=%fused_computation | custom fusion | bytes 1048608 | tf_op jit(solution)/shard_map/jit(_take)/gather | solution.py:62
  11.0 0.9 %broadcast_select_fusion = bf16[8,16,2048]{2,1,0:T(8,128)(2,1)} fusion(bf16[8,16,2048]{2,1,0:T(8,128)(2,1)S(1)} %gather_fusion, pred[8]{0:T(512)(128)(4,1)S(1)} %get-tuple-element.5), kind=kLoop, calls=%fused_computation.4 | loop fusion | flops 262144 | bytes 1048584 | tf_op jit(solution)/shard_map/jit(_take)/select_n | solution.py:62
  11.9 0.0 reduce-scatter.2.cloned.1.call-start
  12.0 4.4 %fusion.2 = f32[256,1024]{1,0:T(8,128)} fusion(bf16[256,2048]{1,0:T(8,128)(2,1)S(1)} %bitcast.25, bf16[2048,1024]{1,0:T(8,128)(2,1)} %param.8), kind=kOutput, calls=%fused_computation.25 | convolution fusion | flops 1073741824 | bytes 6291456 | tf_op jit(solution)/shard_map/dot_general | solution.py:56
  16.4 1.6 %gather_fusion.1 = bf16[8,16,256]{2,1,0:T(8,128)(2,1)S(1)} fusion(bf16[64,16,256]{2,1,0:T(8,128)(2,1)} %param.10, s32[1024]{0:T(1024)S(1)} %pad_clamp_fusion), kind=kCustom, calls=%fused_computation.1 | custom fusion | bytes 131104 | tf_op jit(solution)/shard_map/jit(_take)/gather | solution.py:63
  18.0 0.1 broadcast_select_fusion.1
  18.1 18.1 %all_gather.7 = bf16[32,16,256]{2,1,0:T(8,128)(2,1)S(1)} all-gather(bf16[8,16,256]{2,1,0:T(8,128)(2,1)S(1)} %broadcast_select_fusion.1), channel_id=1, replica_groups=mesh['groups'=2,'inst'=4,'tp'=4] {'inst'}, dimensions={0}, use_global_device_ids=true | all-gather | bytes 327680 | tf_op jit(solution)/shard_map/all_gather | solution.py:67
  36.2 0.1 copy.10
  36.3 0.7 convolution_convert_fusion
  37.1 0.6 copy.11
  37.8 1.2 %multiply_cosine_fusion = (f32[256,64]{1,0:T(8,128)}, f32[256,64]{1,0:T(8,128)}) fusion(f32[64]{0:T(128)S(1)} %compare_select_fusion.2, f32[256]{0:T(256)S(1)} %add_convert_fusion.1), kind=kLoop, calls=%fused_computation.10 | loop fusion | flops 16384 | bytes 132352 | tf_op jit(solution)/shard_map/cos | solution.py:28
  39.1 24.5 %all-gather.2.cloned.1.call-done = bf16[32,16,2048]{2,1,0:T(8,128)(2,1)} async-done(((bf16[8,16,2048]{2,1,0:T(8,128)(2,1)}), bf16[32,16,2048]{2,1,0:T(8,128)(2,1)}) %all-gather.2.cloned.1.call-update) | async-done | bytes 2097168 | tf_op jit(solution)/shard_map/all_gather | solution.py:66
  63.6 2.3 %fusion.3 = f32[512,256]{1,0:T(8,128)S(1)} fusion(bf16[512,2048]{1,0:T(8,128)(2,1)} %bitcast.33, bf16[256,2048]{1,0:T(8,128)(2,1)S(1)} %bitcast.26), kind=kOutput, calls=%fused_computation.26 | convolution fusion | flops 536870912 | bytes 3670016 | tf_op jit(solution)/shard_map/dot_general | solution.py:71
  65.9 0.1 multiply_reduce_fusion
  66.0 11.2 %psum.7 = bf16[256,16]{0,1:T(8,128)(2,1)S(1)} all-reduce(f32[256,16]{0,1:T(8,128)S(1)} %multiply_reduce_fusion), channel_id=1, replica_groups=mesh['groups'=2,'inst'=4,'tp'=4] {'tp'}, use_global_device_ids=true, to_apply=%region_2.3 | all-reduce | flops 4096 | bytes 24576 | tf_op jit(solution)/shard_map/psum | solution.py:86
  77.2 0.1 copy.8
  77.4 0.4 fusion.4
  77.8 0.0 reduce-scatter.2.cloned.1.call-done
  77.8 1.0 %multiply_add_fusion = f32[256,256]{1,0:T(8,128)S(1)} fusion(f32[256,256]{1,0:T(8,128)} %reduce-scatter.2.cloned.1.call-done, bf16[256,1,256]{2,1,0:T(2,128)(2,1)S(1)} %fusion.4), kind=kLoop, calls=%fused_computation.8 | loop fusion | flops 196608 | bytes 655360 | tf_op jit(solution)/shard_map/add | solution.py:93
  78.8 0.1 reshape.142
  78.9 1.4 %subtract_convert_fusion = (bf16[256,2,64]{2,1,0:T(2,128)(2,1)S(1)}, bf16[256,2,64]{2,1,0:T(2,128)(2,1)S(1)}) fusion(f32[256,2,128]{2,1,0:T(2,128)S(1)} %reshape.142, f32[256,64]{1,0:T(8,128)} %get-tuple-element.10, f32[256,64]{1,0:T(8,128)} %get-tuple-element.9), kind=kLoop, calls=%fused_computation.7 | loop fusion | flops 262144 | bytes 524288 | tf_op jit(solution)/shard_map/convert
  80.4 0.4 pad_maximum_fusion
  80.8 0.7 convert_element_type.39
  (15 shorter events, 0.1 us)
Async XLA Ops:
  7.4 4.6 %copy-start = (bf16[2,128,2048]{2,1,0:T(8,128)(2,1)S(1)}, bf16[2,128,2048]{2,1,0:T(8,128)(2,1)}, u32[]{:S(2)}) copy-start(bf16[2,128,2048]{2,1,0:T(8,128)(2,1)} %param.7) | copy-start | bytes 3145732
  7.4 56.2 %all-gather.2.cloned.1.call-start = ((), (), s32[]{:S(2)}) async-start(), calls=%async_computation.2 | async-start | bytes 2621440 | tf_op jit(solution)/shard_map/all_gather | solution.py:66
  11.9 65.9 %reduce-scatter.2.cloned.1.call-start = ((), (), s32[]{:S(2)}) async-start(), calls=%async_computation.1 | async-start | bytes 1310720 | tf_op jit(solution)/shard_map/reduce_scatter | solution.py:57
  16.4 19.9 %copy-start.2 = (s32[128]{0:T(128)S(1)}, s32[128]{0:T(128)}, u32[]{:S(2)}) copy-start(s32[128]{0:T(128)} %param.11) | copy-start | bytes 1540
  37.1 0.7 copy-start.1
Sparse Core Ops, SparseCore 0:
  12.0 51.5 all-gather.1
Sparse Core Ops, SparseCore 1:
  16.5 27.5 reduce-scatter.1
where the time goes:
time: 89.3 us; the launch traced here: 89 us
  blocking collectives  29.3 us (33%)
  waiting for transfers between devices  24.6 us (28%)
  between operations  15 us (17%)
  matrix products  7.93 us (9%)
  local copies, waits for them, and re-layouts  6.11 us (7%)
  other arithmetic  5.96 us (7%)
    all_gather x1, waiting for transfers between devices, on_device(): lax.all_gather(request_down_weight, 'inst', axis=0, tiled=True)  24.5 us
    all_gather x1, blocking collectives, on_device(): lax.all_gather(request_up_weight, 'inst', axis=0, tiled=True)  18.1 us
    psum x1, blocking collectives, on_device(): shrink = lax.psum(chosen, 'tp').astype(jnp.bfloat16)  11.2 us
    dot_general x1, matrix products, on_device(): jnp.dot(flat_rows, key_matrix, preferred_element_type=jnp.float32)  4.44 us
    gather x1, local copies, waits for them, and re-layouts, on_device(): jnp.take(adapter_down_weight, request_pool_rows, axis=0)  2.77 us
    dot_general x1, matrix products, on_device(): lax.dot_general(flat_rows, down_piece, (((1,), (1,)), ((), ())), preferre...  2.33 us
  transfers between devices with their start and end apart: 2, of which 1 were waited for; matrix products, arithmetic and copies ran while one was open for 13% of the time, Pallas kernels for 0%

commit v1 on v0

v1 whole, which is shorter than its diff:
```python
import functools

import jax
import jax.numpy as jnp
import numpy as np
from jax import lax
from jax.experimental import pallas as pl
from jax.experimental.pallas import tpu as pltpu
from jax.sharding import PartitionSpec as P

HEAD = 128
ADAPTER_SCALE = 2.0
ROPE_THETA = 500000.0
MESH_ID = pl.DeviceIdType.MESH


def rope_freqs(head_size):
    pair = np.arange(head_size // 2, dtype=np.float64)
    base = ROPE_THETA ** (-2.0 * pair / head_size)
    wavelen = 2.0 * np.pi / base
    smooth = (8192.0 / wavelen - 1.0) / 3.0
    blended = (1.0 - smooth) * base / 8.0 + smooth * base
    scaled = np.where(wavelen > 8192.0, base / 8.0, blended)
    return np.where(wavelen < 2048.0, base, scaled).astype(np.float32)


def kernel(
    n_inst, n_tp, n_act, rank, pool_rows_ref, slot_ref, len_ref, freq_ref,
    hidden_hbm, key_hbm, down_hbm, up_hbm, out_ref,
    hidden, key, down, up, gath, part, keys_in, score, score_in, cos_tab, sin_tab,
    load_sem, out_right_sem, out_left_sem, in_sem, key_out_sem, key_in_sem, sc_out_sem, sc_in_sem,
):
    me = lax.axis_index("inst")
    tp = lax.axis_index("tp")
    steps, requests, width = hidden.shape
    rows = steps * requests
    local = up.shape[2]
    pool_count = down.shape[0]
    block = n_act * rank

    barrier = pltpu.get_barrier_semaphore()
    for shift in (1, n_inst - 1):
        pl.semaphore_signal(
            barrier, inc=1, device_id={"inst": lax.rem(me + shift, n_inst)}, device_id_type=MESH_ID
        )
    for shift in range(1, n_tp):
        pl.semaphore_signal(
            barrier, inc=1, device_id={"tp": lax.rem(tp + shift, n_tp)}, device_id_type=MESH_ID
        )

    load_down = pltpu.make_async_copy(down_hbm, down, load_sem.at[0])
    load_up = pltpu.make_async_copy(up_hbm, up, load_sem.at[1])
    load_hidden = pltpu.make_async_copy(hidden_hbm, hidden, load_sem.at[2])
    load_key = pltpu.make_async_copy(key_hbm, key, load_sem.at[3])
    load_down.start()
    load_up.start()
    load_hidden.start()
    load_key.start()

    load_down.wait()
    load_up.wait()
    for k in range(n_act):
        row = lax.rem(pool_rows_ref[me * n_act + k], pool_count)
        gath[me, k * rank : (k + 1) * rank, :width] = down[row]
        gath[me, k * rank : (k + 1) * rank, width:] = up[row]

    pl.semaphore_wait(barrier, 2 + n_tp - 1)

    def send_right(owner):
        return pltpu.make_async_remote_copy(
            src_ref=gath.at[owner], dst_ref=gath.at[owner],
            send_sem=out_right_sem.at[owner], recv_sem=in_sem.at[owner],
            device_id={"inst": lax.rem(me + 1, n_inst)}, device_id_type=MESH_ID,
        )

    def send_left(owner):
        return pltpu.make_async_remote_copy(
            src_ref=gath.at[owner], dst_ref=gath.at[owner],
            send_sem=out_left_sem.at[owner], recv_sem=in_sem.at[owner],
            device_id={"inst": lax.rem(me + n_inst - 1, n_inst)}, device_id_type=MESH_ID,
        )

    @pl.when(me + 1 < n_inst)
    def _():
        send_right(me).start()

    @pl.when(me > 0)
    def _():
        send_left(me).start()

    load_hidden.wait()
    load_key.wait()

    def send_keys(shift):
        peer = lax.rem(tp + shift, n_tp)
        return pltpu.make_async_remote_copy(
            src_ref=part.at[shift], dst_ref=keys_in.at[shift],
            send_sem=key_out_sem.at[shift], recv_sem=key_in_sem.at[shift],
            device_id={"tp": peer}, device_id_type=MESH_ID,
        )

    def partial_keys(shift):
        peer = lax.rem(tp + shift, n_tp)
        columns = pl.ds(pl.multiple_of(peer * local, local), local)
        part[shift] = jnp.dot(
            hidden[...].reshape(rows, width), key[:, columns], preferred_element_type=jnp.float32
        )

    for shift in range(1, n_tp):
        partial_keys(shift)
        send_keys(shift).start()
    partial_keys(0)

    slots = jnp.concatenate([slot_ref[...]] * steps, axis=1)

    def add_scores(owner):
        piece = lax.dot_general(
            gath[owner, :, :width], hidden[...].reshape(rows, width),
            (((1,), (1,)), ((), ())), preferred_element_type=jnp.float32,
        )
        total = score[0]
        for k in range(n_act):
            total += jnp.where(
                slots == owner * n_act + k, piece[k * rank : (k + 1) * rank, :], 0.0
            )
        score[0] = total

    score[0] = jnp.zeros((rank, rows), jnp.float32)
    add_scores(me)

    lens = jnp.broadcast_to(len_ref[...].astype(jnp.float32), (HEAD, requests)).T
    lane = lax.broadcasted_iota(jnp.int32, (requests, HEAD), 1)
    for s in range(steps):
        angle = (lens + float(s)) * freq_ref[...]
        sine = jnp.sin(angle)
        cos_tab[s * requests : (s + 1) * requests, :] = jnp.cos(angle)
        sin_tab[s * requests : (s + 1) * requests, :] = jnp.where(lane < HEAD // 2, -sine, sine)

    def step(d, carry):
        low = me - d
        high = me + d

        @pl.when(low >= 0)
        def _():
            send_right(low).wait_recv()

            @pl.when(me + 1 < n_inst)
            def _():
                send_right(low).start()

        @pl.when(high < n_inst)
        def _():
            send_left(high).wait_recv()

            @pl.when(me > 0)
            def _():
                send_left(high).start()

        @pl.when(low >= 0)
        def _():
            add_scores(low)

        @pl.when(high < n_inst)
        def _():
            add_scores(high)

        return carry

    lax.fori_loop(1, n_inst, step, 0)

    def send_score(shift):
        return pltpu.make_async_remote_copy(
            src_ref=score.at[0], dst_ref=score_in.at[shift],
            send_sem=sc_out_sem.at[shift], recv_sem=sc_in_sem.at[shift],
            device_id={"tp": lax.rem(tp + shift, n_tp)}, device_id_type=MESH_ID,
        )

    for shift in range(1, n_tp):
        send_score(shift).start()

    plain = part[0]
    for shift in range(1, n_tp):
        send_keys(shift).wait_recv()
        plain += keys_in[shift]

    shrink = score[0]
    for shift in range(1, n_tp):
        send_score(shift).wait_recv()
        shrink += score_in[shift]
    shrink = shrink.astype(jnp.bfloat16).astype(jnp.float32)

    def add_update(owner, total):
        spread = jnp.concatenate(
            [jnp.where(slots == owner * n_act + k, shrink, 0.0) for k in range(n_act)], axis=0
        )
        return total + lax.dot_general(
            spread.astype(jnp.bfloat16), gath[owner, :, width:],
            (((0,), (0,)), ((), ())), preferred_element_type=jnp.float32,
        )

    update = lax.fori_loop(0, n_inst, add_update, jnp.zeros((rows, local), jnp.float32))
    mixed = plain + ADAPTER_SCALE * update.astype(jnp.bfloat16).astype(jnp.float32)
    for h in range(local // HEAD):
        values = mixed[:, h * HEAD : (h + 1) * HEAD]
        turned = values * cos_tab[...] + pltpu.roll(values, HEAD // 2, 1) * sin_tab[...]
        out_ref[:, :, h * HEAD : (h + 1) * HEAD] = turned.astype(jnp.bfloat16).reshape(
            steps, requests, HEAD
        )

    for shift in range(1, n_tp):
        send_keys(shift).wait_send()
        send_score(shift).wait_send()

    def drain(owner, carry):
        @pl.when((owner <= me) & (me + 1 < n_inst))
        def _():
            send_right(owner).wait_send()

        @pl.when((owner >= me) & (me > 0))
        def _():
            send_left(owner).wait_send()

        return carry

    lax.fori_loop(0, n_inst, drain, 0)


def on_device(
    hidden, key_matrix, down_weight, up_weight, request_slot, pool_rows, lengths
):
    n_inst = lax.axis_size("inst")
    n_tp = lax.axis_size("tp")
    steps, requests, width = hidden.shape
    _, rank, local = up_weight.shape
    n_act = pool_rows.shape[0] // n_inst
    rows = steps * requests
    block = n_act * rank
    freqs = rope_freqs(HEAD)
    vmem = pl.BlockSpec(memory_space=pltpu.VMEM)
    hbm = pl.BlockSpec(memory_space=pl.ANY)
    return pl.pallas_call(
        functools.partial(kernel, n_inst, n_tp, n_act, rank),
        out_shape=jax.ShapeDtypeStruct((steps, requests, local), jnp.bfloat16),
        in_specs=[pl.BlockSpec(memory_space=pltpu.SMEM), vmem, vmem, vmem, hbm, hbm, hbm, hbm],
        out_specs=vmem,
        scratch_shapes=[
            pltpu.VMEM(hidden.shape, jnp.bfloat16),
            pltpu.VMEM(key_matrix.shape, jnp.bfloat16),
            pltpu.VMEM(down_weight.shape, jnp.bfloat16),
            pltpu.VMEM(up_weight.shape, jnp.bfloat16),
            pltpu.VMEM((n_inst, block, width + local), jnp.bfloat16),
            pltpu.VMEM((n_tp, rows, local), jnp.float32),
            pltpu.VMEM((n_tp, rows, local), jnp.float32),
            pltpu.VMEM((1, rank, rows), jnp.float32),
            pltpu.VMEM((n_tp, rank, rows), jnp.float32),
            pltpu.VMEM((rows, HEAD), jnp.float32),
            pltpu.VMEM((rows, HEAD), jnp.float32),
            pltpu.SemaphoreType.DMA((4,)),
            pltpu.SemaphoreType.DMA((n_inst,)),
            pltpu.SemaphoreType.DMA((n_inst,)),
            pltpu.SemaphoreType.DMA((n_inst,)),
            pltpu.SemaphoreType.DMA((n_tp,)),
            pltpu.SemaphoreType.DMA((n_tp,)),
            pltpu.SemaphoreType.DMA((n_tp,)),
            pltpu.SemaphoreType.DMA((n_tp,)),
        ],
        compiler_params=pltpu.CompilerParams(
            collective_id=0, has_side_effects=True, vmem_limit_bytes=48 * 1024 * 1024
        ),
        name="lora_keys",
    )(
        pool_rows,
        request_slot.reshape(1, requests),
        lengths.reshape(1, requests),
        jnp.asarray(np.concatenate([freqs, freqs]).reshape(1, HEAD)),
        hidden,
        key_matrix,
        down_weight,
        up_weight,
    )


def solution(mesh):
    placed = (
        P(None, ("groups", "inst"), "tp"),
        P("tp", None),
        P("inst", None, "tp"),
        P("inst", None, "tp"),
        P(("groups", "inst")),
        P("groups"),
        P(("groups", "inst")),
    )
    return jax.shard_map(
        on_device,
        mesh=mesh,
        in_specs=placed,
        out_specs=P(None, ("groups", "inst"), "tp"),
        check_vma=False,
    )
```

time: 89.3 us -> 60.4 us (0.68)
  Pallas kernels: 0 us -> 52.3 us
  blocking collectives: 29.3 us -> 0 us
  waiting for transfers between devices: 24.6 us -> 0 us
  between operations: 15 us -> 0.02 us
  matrix products: 7.93 us -> 0 us
  other arithmetic: 5.96 us -> 0 us
  local copies, waits for them, and re-layouts: 6.11 us -> 7.73 us
    pallas_call x0 -> x1, Pallas kernels: none -> 52.3 us  [on_device(): pl.pallas_call(functools.partial(kernel, n_inst, n_tp, n_act, rank), out_...]
    all_gather x1 -> x0, waiting for transfers between devices: 24.5 us -> none  [on_device(): lax.all_gather(request_down_weight, 'inst', axis=0, tiled=True)]
    all_gather x1 -> x0, blocking collectives: 18.1 us -> none  [on_device(): lax.all_gather(request_up_weight, 'inst', axis=0, tiled=True)]
    psum x1 -> x0, blocking collectives: 11.2 us -> none  [on_device(): shrink = lax.psum(chosen, 'tp').astype(jnp.bfloat16)]
    dot_general x4 -> x0, matrix products: 7.93 us -> none  [the longest x1 4.44 us: on_device(): jnp.dot(flat_rows, key_matrix, preferred_element_type=jnp.float32)]
    unnamed x8 -> x15, local copies, waits for them, and re-layouts: 0.74 us -> 7.73 us
    gather x2 -> x0, local copies, waits for them, and re-layouts: 4.36 us -> none  [the longest x1 2.77 us: on_device(): jnp.take(adapter_down_weight, request_pool_rows, axis=0)]
    another operation x1 -> x0, other arithmetic: 1.44 us -> none
  transfers between devices with their start and end apart: 2 -> 0, of which waited for: 1 -> 0; matrix products, arithmetic and copies ran while one was open for 13% -> 0% of each run, Pallas kernels for 0% -> 0%
where the time goes in v1:
time: 60.4 us; the launch traced here: 60.1 us
  Pallas kernels  52.3 us (87%)
  local copies, waits for them, and re-layouts  7.73 us (13%)
    pallas_call x1, Pallas kernels, on_device(): pl.pallas_call(functools.partial(kernel, n_inst, n_tp, n_act, rank), out_...  52.3 us
    unnamed x15, local copies, waits for them, and re-layouts  7.73 us

profile of v1, /device:TPU:0, one launch (start us, length us, event | category | flops | bytes accessed | tf_op | source)
XLA Modules:
  0.0 60.1 jit_solution(1772093009947101707)
XLA Ops:
  0.0 0.0 copy-start
  0.0 2.2 %copy-done = bf16[2048,1024]{1,0:T(8,128)(2,1)S(1)} copy-done((bf16[2048,1024]{1,0:T(8,128)(2,1)S(1)}, bf16[2048,1024]{1,0:T(8,128)(2,1)}, u32[]{:S(2)}) %copy-start) | copy-done | bytes 4194328
  2.2 0.0 copy-start.1
  2.2 1.2 %copy-done.1 = bf16[2,128,2048]{2,1,0:T(8,128)(2,1)S(1)} copy-done((bf16[2,128,2048]{2,1,0:T(8,128)(2,1)S(1)}, bf16[2,128,2048]{2,1,0:T(8,128)(2,1)}, u32[]{:S(2)}) %copy-start.1) | copy-done | bytes 1048600
  3.4 0.0 copy-start.2
  3.4 1.0 %copy-done.2 = bf16[64,16,256]{2,1,0:T(8,128)(2,1)S(1)} copy-done((bf16[64,16,256]{2,1,0:T(8,128)(2,1)S(1)}, bf16[64,16,256]{2,1,0:T(8,128)(2,1)}, u32[]{:S(2)}) %copy-start.2) | copy-done | bytes 524312
  4.5 0.0 copy-start.3
  4.5 0.7 %copy-done.3 = s32[32]{0:T(128)S(1)} copy-done((s32[32]{0:T(128)S(1)}, s32[32]{0:T(128)}, u32[]{:S(2)}) %copy-start.3) | copy-done | bytes 152
  5.1 0.0 copy-start.4
  5.1 0.7 %copy-done.4 = s32[128]{0:T(128)S(1)} copy-done((s32[128]{0:T(128)S(1)}, s32[128]{0:T(128)}, u32[]{:S(2)}) %copy-start.4) | copy-done | bytes 536
  5.8 0.0 copy-start.5
  5.8 0.7 %copy-done.5 = s32[128]{0:T(128)S(1)} copy-done((s32[128]{0:T(128)S(1)}, s32[128]{0:T(128)}, u32[]{:S(2)}) %copy-start.5) | copy-done | bytes 536
  6.4 0.0 copy-start.6
  6.4 0.7 %copy-done.6 = f32[1,128]{1,0:T(1,128)S(1)} copy-done((f32[1,128]{1,0:T(1,128)S(1)}, f32[1,128]{1,0:T(1,128)}, u32[]{:S(2)}) %copy-start.6) | copy-done | bytes 536
  7.1 52.3 %lora_keys.1 = bf16[2,128,256]{2,1,0:T(8,128)(2,1)S(1)} custom-call(s32[32]{0:T(128)S(1)} %copy-done.3, s32[1,128]{1,0:T(1,128)S(1)} %bitcast.2, s32[1,128]{1,0:T(1,128)S(1)} %bitcast.3, f32[1,128]{1,0:T(1,128)S(1)} %copy-done.6, bf16[2,128,2048]{2,1,0:T(8,128)(2,1)S(1)} %copy-done.1, bf16[2048,1024]{1,0:T(8,128)(2,1)S(1)} %copy-done, ...), custom_call_target="tpu_custom_call" | custom-call | tf_op jit(solution)/shard_map/lora_keys/pallas_call | solution.py:241
  59.4 0.7 %copy.10 = bf16[2,128,256]{2,1,0:T(8,128)(2,1)} copy(bf16[2,128,256]{2,1,0:T(8,128)(2,1)S(1)} %lora_keys.1) | data formatting | bytes 262144
Async XLA Ops:
  0.0 2.2 %copy-start = (bf16[2048,1024]{1,0:T(8,128)(2,1)S(1)}, bf16[2048,1024]{1,0:T(8,128)(2,1)}, u32[]{:S(2)}) copy-start(bf16[2048,1024]{1,0:T(8,128)(2,1)} %key_hbm.1) | copy-start | bytes 12582916
  2.2 1.2 %copy-start.1 = (bf16[2,128,2048]{2,1,0:T(8,128)(2,1)S(1)}, bf16[2,128,2048]{2,1,0:T(8,128)(2,1)}, u32[]{:S(2)}) copy-start(bf16[2,128,2048]{2,1,0:T(8,128)(2,1)} %hidden_hbm.1) | copy-start | bytes 3145732
  3.4 1.0 %copy-start.2 = (bf16[64,16,256]{2,1,0:T(8,128)(2,1)S(1)}, bf16[64,16,256]{2,1,0:T(8,128)(2,1)}, u32[]{:S(2)}) copy-start(bf16[64,16,256]{2,1,0:T(8,128)(2,1)} %up_hbm.1) | copy-start | bytes 1572868
  4.5 0.7 %copy-start.3 = (s32[32]{0:T(128)S(1)}, s32[32]{0:T(128)}, u32[]{:S(2)}) copy-start(s32[32]{0:T(128)} %pool_rows_ref.1) | copy-start | bytes 388
  5.1 0.7 %copy-start.4 = (s32[128]{0:T(128)S(1)}, s32[128]{0:T(128)}, u32[]{:S(2)}) copy-start(s32[128]{0:T(128)} %param.12) | copy-start | bytes 1540
  5.8 0.7 %copy-start.5 = (s32[128]{0:T(128)S(1)}, s32[128]{0:T(128)}, u32[]{:S(2)}) copy-start(s32[128]{0:T(128)} %param.14) | copy-start | bytes 1540
  6.4 0.7 %copy-start.6 = (f32[1,128]{1,0:T(1,128)S(1)}, f32[1,128]{1,0:T(1,128)}, u32[]{:S(2)}) copy-start(f32[1,128]{1,0:T(1,128)} %constant.2.clone.freq_ref) | copy-start | bytes 1540

commit v2 on v1

v2 whole, which is shorter than its diff:
```python
import functools

import jax
import jax.numpy as jnp
import numpy as np
from jax import lax
from jax.experimental import pallas as pl
from jax.experimental.pallas import tpu as pltpu
from jax.sharding import PartitionSpec as P

HEAD = 128
ADAPTER_SCALE = 2.0
ROPE_THETA = 500000.0
MESH_ID = pl.DeviceIdType.MESH


def rope_freqs(head_size):
    pair = np.arange(head_size // 2, dtype=np.float64)
    base = ROPE_THETA ** (-2.0 * pair / head_size)
    wavelen = 2.0 * np.pi / base
    smooth = (8192.0 / wavelen - 1.0) / 3.0
    blended = (1.0 - smooth) * base / 8.0 + smooth * base
    scaled = np.where(wavelen > 8192.0, base / 8.0, blended)
    return np.where(wavelen < 2048.0, base, scaled).astype(np.float32)


def kernel(
    n_inst, n_tp, n_act, rank, pool_rows_hbm, slot_hbm, len_hbm, freq_hbm,
    hidden_hbm, key_hbm, down_hbm, up_hbm, out_ref,
    pool_rows, slot, length, freq, hidden, key, down, up, low_half, high_half, guest, guest_slot,
    part, keys_in, score, help_out, help_in, score_in, cos_tab, sin_tab,
    small_sem, load_sem, out_right_sem, out_left_sem, in_sem, guest_out_sem, guest_in_sem,
    help_out_sem, help_in_sem, key_out_sem, key_in_sem, sc_out_sem, sc_in_sem,
):
    me = lax.axis_index("inst")
    tp = lax.axis_index("tp")
    _, steps, requests, half = hidden.shape
    rows = steps * requests
    local = up.shape[2]
    pool_count = down.shape[0]
    last = n_inst - 1
    is_end = (me == 0) | (me == last)

    load_down = pltpu.make_async_copy(down_hbm, down, load_sem.at[0])
    load_up = pltpu.make_async_copy(up_hbm, up, load_sem.at[1])
    load_hidden = [
        pltpu.make_async_copy(
            hidden_hbm.at[:, :, pl.ds(h * half, half)], hidden.at[h], load_sem.at[2 + h]
        )
        for h in range(2)
    ]
    load_key = pltpu.make_async_copy(key_hbm, key, load_sem.at[4])
    load_small = [
        pltpu.make_async_copy(src, dst, small_sem.at[i])
        for i, (src, dst) in enumerate(
            ((pool_rows_hbm, pool_rows), (slot_hbm, slot), (len_hbm, length), (freq_hbm, freq))
        )
    ]
    for copy in load_small:
        copy.start()
    load_down.start()
    load_up.start()
    for copy in load_hidden:
        copy.start()
    load_key.start()

    barrier = pltpu.get_barrier_semaphore()
    for shift in (1, n_inst - 1):
        pl.semaphore_signal(
            barrier, inc=1, device_id={"inst": lax.rem(me + shift, n_inst)}, device_id_type=MESH_ID
        )
    for shift in range(1, n_tp):
        pl.semaphore_signal(
            barrier, inc=1, device_id={"tp": lax.rem(tp + shift, n_tp)}, device_id_type=MESH_ID
        )

    for copy in load_small:
        copy.wait()
    load_down.wait()
    load_up.wait()
    for k in range(n_act):
        row = lax.rem(pool_rows[me * n_act + k], pool_count)
        ranks = slice(k * rank, (k + 1) * rank)
        low_half[me, ranks, :half] = down[row, :, :half]
        low_half[me, ranks, half:] = up[row]
        high_half[me, ranks, :] = down[row, :, half:]

    pl.semaphore_wait(barrier, 2 + n_tp - 1)

    right = {"inst": lax.rem(me + 1, n_inst)}
    left = {"inst": lax.rem(me + n_inst - 1, n_inst)}

    def remote(src, dst, send_sem, recv_sem, device):
        return pltpu.make_async_remote_copy(
            src_ref=src, dst_ref=dst, send_sem=send_sem, recv_sem=recv_sem,
            device_id=device, device_id_type=MESH_ID,
        )

    def hop(h, owner, sems, device):
        buffer = high_half if h else low_half
        return remote(
            buffer.at[owner], buffer.at[owner], sems.at[h, owner], in_sem.at[h, owner], device
        )

    def go_right(h, owner):
        @pl.when(me + 1 < (last if h else n_inst))
        def _():
            hop(h, owner, out_right_sem, right).start()

    def go_left(h, owner):
        @pl.when(me > (1 if h else 0))
        def _():
            hop(h, owner, out_left_sem, left).start()

    def arrive(h, owner):
        hop(h, owner, out_right_sem, right).wait_recv()

    for h in range(2):
        go_right(h, me)
        go_left(h, me)

    for copy in load_hidden:
        copy.wait()
    load_key.wait()

    def send_keys(shift):
        return remote(
            part.at[shift], keys_in.at[shift], key_out_sem.at[shift], key_in_sem.at[shift],
            {"tp": lax.rem(tp + shift, n_tp)},
        )

    def partial_keys(shift):
        peer = lax.rem(tp + shift, n_tp)
        columns = pl.ds(pl.multiple_of(peer * local, local), local)
        part[shift] = jnp.dot(
            hidden[0].reshape(rows, half), key[:half, columns], preferred_element_type=jnp.float32
        ) + jnp.dot(
            hidden[1].reshape(rows, half), key[half:, columns], preferred_element_type=jnp.float32
        )

    for shift in range(1, n_tp):
        partial_keys(shift)
        send_keys(shift).start()
    partial_keys(0)

    slots = jnp.concatenate([slot[...]] * steps, axis=1)

    def pick(total, weights, values, wanted, owner):
        piece = lax.dot_general(
            weights, values, (((1,), (1,)), ((), ())), preferred_element_type=jnp.float32
        )
        for k in range(n_act):
            total += jnp.where(
                wanted == owner * n_act + k, piece[k * rank : (k + 1) * rank, :], 0.0
            )
        return total

    def add_low(owner):
        score[...] = pick(
            score[...], low_half[owner, :, :half], hidden[0].reshape(rows, half), slots, owner
        )

    def add_high(owner):
        score[...] = pick(
            score[...], high_half[owner], hidden[1].reshape(rows, half), slots, owner
        )

    score[...] = jnp.zeros((rank, rows), jnp.float32)
    add_low(me)
    add_high(me)

    lens = jnp.broadcast_to(length[...].astype(jnp.float32), (HEAD, requests)).T
    lane = lax.broadcasted_iota(jnp.int32, (requests, HEAD), 1)
    for s in range(steps):
        angle = (lens + float(s)) * freq[...]
        sine = jnp.sin(angle)
        cos_tab[s * requests : (s + 1) * requests, :] = jnp.cos(angle)
        sin_tab[s * requests : (s + 1) * requests, :] = jnp.where(lane < HEAD // 2, -sine, sine)

    ends = ((0, 0, 1, right), (1, last, last - 1, left))

    def send_guest(e, device):
        return (
            remote(hidden.at[1], guest.at[e], guest_out_sem.at[e, 0], guest_in_sem.at[e, 0], device),
            remote(slot, guest_slot.at[e], guest_out_sem.at[e, 1], guest_in_sem.at[e, 1], device),
        )

    for e, end, _, device in ends:
        sems = out_left_sem if e else out_right_sem

        @pl.when(me == end)
        def _():
            hop(0, me, sems, device).wait_send()
            if n_inst > 2:
                hop(1, me, sems, device).wait_send()
            for copy in send_guest(e, device):
                copy.start()

    def step(d, carry):
        lower = me - d
        upper = me + d
        sides = ((lower, lower >= 0, go_right), (upper, upper < n_inst, go_left))
        for owner, there, go_on in sides:

            @pl.when(there)
            def _():
                arrive(0, owner)
                go_on(0, owner)

        for owner, there, go_on in sides:

            @pl.when(there & jnp.logical_not(is_end))
            def _():
                arrive(1, owner)
                go_on(1, owner)
                add_high(owner)

        for owner, there, go_on in sides:

            @pl.when(there)
            def _():
                add_low(owner)

        return carry

    lax.fori_loop(1, n_inst, step, 0)

    def send_help(e, device):
        return remote(help_out.at[e], help_in, help_out_sem.at[e], help_in_sem.at[e], device)

    for e, end, helper, device in ends:
        back = left if e == 0 else right

        @pl.when(me == helper)
        def _():
            for copy in send_guest(e, device):
                copy.wait_recv()
            wanted = jnp.concatenate([guest_slot[e]] * steps, axis=1)

            def add_guest(i, total):
                owner = i + 1 - e
                return pick(
                    total, high_half[owner], guest[e].reshape(rows, half), wanted, owner
                )

            help_out[e] = lax.fori_loop(
                0, n_inst - 1, add_guest, jnp.zeros((rank, rows), jnp.float32)
            )
            send_help(e, back).start()

    for e, end, helper, device in ends:

        @pl.when(me == end)
        def _():
            send_help(e, device).wait_recv()
            score[...] += help_in[...]

    def send_score(shift):
        return remote(
            score, score_in.at[shift], sc_out_sem.at[shift], sc_in_sem.at[shift],
            {"tp": lax.rem(tp + shift, n_tp)},
        )

    for shift in range(1, n_tp):
        send_score(shift).start()

    for shift in range(1, n_tp):
        send_keys(shift).wait_recv()
        part[0] += keys_in[shift]

    shrink = score[...]
    for shift in range(1, n_tp):
        send_score(shift).wait_recv()
        shrink += score_in[shift]
    shrink = shrink.astype(jnp.bfloat16).astype(jnp.float32)

    def add_update(owner, total):
        spread = jnp.concatenate(
            [jnp.where(slots == owner * n_act + k, shrink, 0.0) for k in range(n_act)], axis=0
        )
        return total + lax.dot_general(
            spread.astype(jnp.bfloat16), low_half[owner, :, half:],
            (((0,), (0,)), ((), ())), preferred_element_type=jnp.float32,
        )

    update = lax.fori_loop(0, n_inst, add_update, jnp.zeros((rows, local), jnp.float32))
    mixed = part[0] + ADAPTER_SCALE * update.astype(jnp.bfloat16).astype(jnp.float32)
    for h in range(local // HEAD):
        values = mixed[:, h * HEAD : (h + 1) * HEAD]
        turned = values * cos_tab[...] + pltpu.roll(values, HEAD // 2, 1) * sin_tab[...]
        out_ref[:, :, h * HEAD : (h + 1) * HEAD] = turned.astype(jnp.bfloat16).reshape(
            steps, requests, HEAD
        )

    for shift in range(1, n_tp):
        send_keys(shift).wait_send()
        send_score(shift).wait_send()
    for e, end, helper, device in ends:

        @pl.when(me == end)
        def _():
            for copy in send_guest(e, device):
                copy.wait_send()

        @pl.when(me == helper)
        def _():
            send_help(e, device).wait_send()

    def drain(owner, carry):
        for h in range(2):
            @pl.when((owner <= me) & (me + 1 < (last if h else n_inst)) & (me > 0))
            def _():
                hop(h, owner, out_right_sem, right).wait_send()

            @pl.when((owner >= me) & (me > (1 if h else 0)) & (me < last))
            def _():
                hop(h, owner, out_left_sem, left).wait_send()

        return carry

    lax.fori_loop(0, n_inst, drain, 0)


def on_device(
    hidden, key_matrix, down_weight, up_weight, request_slot, pool_rows, lengths
):
    n_inst = lax.axis_size("inst")
    n_tp = lax.axis_size("tp")
    steps, requests, width = hidden.shape
    _, rank, local = up_weight.shape
    n_act = pool_rows.shape[0] // n_inst
    rows = steps * requests
    block = n_act * rank
    freqs = rope_freqs(HEAD)
    half = width // 2
    vmem = pl.BlockSpec(memory_space=pltpu.VMEM)
    hbm = pl.BlockSpec(memory_space=pltpu.HBM)
    return pl.pallas_call(
        functools.partial(kernel, n_inst, n_tp, n_act, rank),
        out_shape=jax.ShapeDtypeStruct((steps, requests, local), jnp.bfloat16),
        in_specs=[hbm] * 8,
        out_specs=vmem,
        scratch_shapes=[
            pltpu.SMEM(pool_rows.shape, jnp.int32),
            pltpu.VMEM((1, requests), jnp.int32),
            pltpu.VMEM((1, requests), jnp.int32),
            pltpu.VMEM((1, HEAD), jnp.float32),
            pltpu.VMEM((2, steps, requests, half), jnp.bfloat16),
            pltpu.VMEM(key_matrix.shape, jnp.bfloat16),
            pltpu.VMEM(down_weight.shape, jnp.bfloat16),
            pltpu.VMEM(up_weight.shape, jnp.bfloat16),
            pltpu.VMEM((n_inst, block, half + local), jnp.bfloat16),
            pltpu.VMEM((n_inst, block, half), jnp.bfloat16),
            pltpu.VMEM((2, steps, requests, half), jnp.bfloat16),
            pltpu.VMEM((2, 1, requests), jnp.int32),
            pltpu.VMEM((n_tp, rows, local), jnp.float32),
            pltpu.VMEM((n_tp, rows, local), jnp.float32),
            pltpu.VMEM((rank, rows), jnp.float32),
            pltpu.VMEM((2, rank, rows), jnp.float32),
            pltpu.VMEM((rank, rows), jnp.float32),
            pltpu.VMEM((n_tp, rank, rows), jnp.float32),
            pltpu.VMEM((rows, HEAD), jnp.float32),
            pltpu.VMEM((rows, HEAD), jnp.float32),
            pltpu.SemaphoreType.DMA((4,)),
            pltpu.SemaphoreType.DMA((5,)),
            pltpu.SemaphoreType.DMA((2, n_inst)),
            pltpu.SemaphoreType.DMA((2, n_inst)),
            pltpu.SemaphoreType.DMA((2, n_inst)),
            pltpu.SemaphoreType.DMA((2, 2)),
            pltpu.SemaphoreType.DMA((2, 2)),
            pltpu.SemaphoreType.DMA((2,)),
            pltpu.SemaphoreType.DMA((2,)),
            pltpu.SemaphoreType.DMA((n_tp,)),
            pltpu.SemaphoreType.DMA((n_tp,)),
            pltpu.SemaphoreType.DMA((n_tp,)),
            pltpu.SemaphoreType.DMA((n_tp,)),
        ],
        compiler_params=pltpu.CompilerParams(
            collective_id=0, has_side_effects=True, vmem_limit_bytes=48 * 1024 * 1024
        ),
        name="lora_keys",
    )(
        pool_rows,
        request_slot.reshape(1, requests),
        lengths.reshape(1, requests),
        jnp.asarray(np.concatenate([freqs, freqs]).reshape(1, HEAD)),
        hidden,
        key_matrix,
        down_weight,
        up_weight,
    )


def solution(mesh):
    placed = (
        P(None, ("groups", "inst"), "tp"),
        P("tp", None),
        P("inst", None, "tp"),
        P("inst", None, "tp"),
        P(("groups", "inst")),
        P("groups"),
        P(("groups", "inst")),
    )
    return jax.shard_map(
        on_device,
        mesh=mesh,
        in_specs=placed,
        out_specs=P(None, ("groups", "inst"), "tp"),
        check_vma=False,
    )
```

time: 60.4 us -> 49.1 us (0.81)
  Pallas kernels: 52.3 us -> 41 us
    pallas_call x1, Pallas kernels: 52.3 us -> 41 us  [on_device(): pl.pallas_call(functools.partial(kernel, n_inst, n_tp, n_act, rank), out_...]
where the time goes in v2:
time: 49.1 us; the launch traced here: 48.8 us
  Pallas kernels  41 us (84%)
  local copies, waits for them, and re-layouts  7.73 us (16%)
    pallas_call x1, Pallas kernels, on_device(): pl.pallas_call(functools.partial(kernel, n_inst, n_tp, n_act, rank), out_...  41 us
    unnamed x15, local copies, waits for them, and re-layouts  7.73 us

profile of v2, /device:TPU:0, one launch (start us, length us, event | category | flops | bytes accessed | tf_op | source)
XLA Modules:
  0.0 48.8 jit_solution(10894620463562482119)
XLA Ops:
  0.0 0.0 copy-start
  0.0 2.2 %copy-done = bf16[2048,1024]{1,0:T(8,128)(2,1)S(1)} copy-done((bf16[2048,1024]{1,0:T(8,128)(2,1)S(1)}, bf16[2048,1024]{1,0:T(8,128)(2,1)}, u32[]{:S(2)}) %copy-start) | copy-done | bytes 4194328
  2.2 0.0 copy-start.1
  2.2 1.2 %copy-done.1 = bf16[2,128,2048]{2,1,0:T(8,128)(2,1)S(1)} copy-done((bf16[2,128,2048]{2,1,0:T(8,128)(2,1)S(1)}, bf16[2,128,2048]{2,1,0:T(8,128)(2,1)}, u32[]{:S(2)}) %copy-start.1) | copy-done | bytes 1048600
  3.4 0.0 copy-start.2
  3.4 1.0 %copy-done.2 = bf16[64,16,256]{2,1,0:T(8,128)(2,1)S(1)} copy-done((bf16[64,16,256]{2,1,0:T(8,128)(2,1)S(1)}, bf16[64,16,256]{2,1,0:T(8,128)(2,1)}, u32[]{:S(2)}) %copy-start.2) | copy-done | bytes 524312
  4.5 0.0 copy-start.3
  4.5 0.7 %copy-done.3 = s32[32]{0:T(128)S(1)} copy-done((s32[32]{0:T(128)S(1)}, s32[32]{0:T(128)}, u32[]{:S(2)}) %copy-start.3) | copy-done | bytes 152
  5.1 0.0 copy-start.4
  5.1 0.7 %copy-done.4 = s32[128]{0:T(128)S(1)} copy-done((s32[128]{0:T(128)S(1)}, s32[128]{0:T(128)}, u32[]{:S(2)}) %copy-start.4) | copy-done | bytes 536
  5.8 0.0 copy-start.5
  5.8 0.7 %copy-done.5 = s32[128]{0:T(128)S(1)} copy-done((s32[128]{0:T(128)S(1)}, s32[128]{0:T(128)}, u32[]{:S(2)}) %copy-start.5) | copy-done | bytes 536
  6.4 0.0 copy-start.6
  6.4 0.7 %copy-done.6 = f32[1,128]{1,0:T(1,128)S(1)} copy-done((f32[1,128]{1,0:T(1,128)S(1)}, f32[1,128]{1,0:T(1,128)}, u32[]{:S(2)}) %copy-start.6) | copy-done | bytes 536
  7.1 41.0 %lora_keys.1 = bf16[2,128,256]{2,1,0:T(8,128)(2,1)S(1)} custom-call(s32[32]{0:T(128)S(1)} %copy-done.3, s32[1,128]{1,0:T(1,128)S(1)} %bitcast.2, s32[1,128]{1,0:T(1,128)S(1)} %bitcast.3, f32[1,128]{1,0:T(1,128)S(1)} %copy-done.6, bf16[2,128,2048]{2,1,0:T(8,128)(2,1)S(1)} %copy-done.1, bf16[2048,1024]{1,0:T(8,128)(2,1)S(1)} %copy-done, ...), custom_call_target="tpu_custom_call" | custom-call | tf_op jit(solution)/shard_map/lora_keys/pallas_call | solution.py:338
  48.1 0.7 %copy.10 = bf16[2,128,256]{2,1,0:T(8,128)(2,1)} copy(bf16[2,128,256]{2,1,0:T(8,128)(2,1)S(1)} %lora_keys.1) | data formatting | bytes 262144
Async XLA Ops:
  0.0 2.2 %copy-start = (bf16[2048,1024]{1,0:T(8,128)(2,1)S(1)}, bf16[2048,1024]{1,0:T(8,128)(2,1)}, u32[]{:S(2)}) copy-start(bf16[2048,1024]{1,0:T(8,128)(2,1)} %key_hbm.1) | copy-start | bytes 12582916
  2.2 1.2 %copy-start.1 = (bf16[2,128,2048]{2,1,0:T(8,128)(2,1)S(1)}, bf16[2,128,2048]{2,1,0:T(8,128)(2,1)}, u32[]{:S(2)}) copy-start(bf16[2,128,2048]{2,1,0:T(8,128)(2,1)} %hidden_hbm.1) | copy-start | bytes 3145732
  3.4 1.0 %copy-start.2 = (bf16[64,16,256]{2,1,0:T(8,128)(2,1)S(1)}, bf16[64,16,256]{2,1,0:T(8,128)(2,1)}, u32[]{:S(2)}) copy-start(bf16[64,16,256]{2,1,0:T(8,128)(2,1)} %up_hbm.1) | copy-start | bytes 1572868
  4.5 0.7 %copy-start.3 = (s32[32]{0:T(128)S(1)}, s32[32]{0:T(128)}, u32[]{:S(2)}) copy-start(s32[32]{0:T(128)} %pool_rows_hbm.1) | copy-start | bytes 388
  5.1 0.7 %copy-start.4 = (s32[128]{0:T(128)S(1)}, s32[128]{0:T(128)}, u32[]{:S(2)}) copy-start(s32[128]{0:T(128)} %param.12) | copy-start | bytes 1540
  5.8 0.7 %copy-start.5 = (s32[128]{0:T(128)S(1)}, s32[128]{0:T(128)}, u32[]{:S(2)}) copy-start(s32[128]{0:T(128)} %param.14) | copy-start | bytes 1540
  6.4 0.7 %copy-start.6 = (f32[1,128]{1,0:T(1,128)S(1)}, f32[1,128]{1,0:T(1,128)}, u32[]{:S(2)}) copy-start(f32[1,128]{1,0:T(1,128)} %constant.2.clone.freq_hbm) | copy-start | bytes 1540

commit v3 on v2

--- a/solution.py
+++ b/solution.py
@@ -28,7 +28,7 @@
     n_inst, n_tp, n_act, rank, pool_rows_hbm, slot_hbm, len_hbm, freq_hbm,
     hidden_hbm, key_hbm, down_hbm, up_hbm, out_ref,
     pool_rows, slot, length, freq, hidden, key, down, up, low_half, high_half, guest, guest_slot,
-    part, keys_in, score, help_out, help_in, score_in, cos_tab, sin_tab,
+    part, keys_in, score, total_score, help_out, help_in, score_in, cos_tab, sin_tab,
     small_sem, load_sem, out_right_sem, out_left_sem, in_sem, guest_out_sem, guest_in_sem,
     help_out_sem, help_in_sem, key_out_sem, key_in_sem, sc_out_sem, sc_in_sem,
 ):
@@ -60,9 +60,6 @@
         copy.start()
     load_down.start()
     load_up.start()
-    for copy in load_hidden:
-        copy.start()
-    load_key.start()
 
     barrier = pltpu.get_barrier_semaphore()
     for shift in (1, n_inst - 1):
@@ -74,10 +71,28 @@
             barrier, inc=1, device_id={"tp": lax.rem(tp + shift, n_tp)}, device_id_type=MESH_ID
         )
 
+    ends = (
+        (0, 0, 1, {"inst": lax.rem(me + 1, n_inst)}),
+        (1, last, last - 1, {"inst": lax.rem(me + n_inst - 1, n_inst)}),
+    )
+    for e, end, helper, _ in ends:
+        for here, there in ((end, helper), (helper, end)):
+
+            @pl.when(me == here)
+            def _():
+                for shift in range(1, n_tp):
+                    pl.semaphore_signal(
+                        barrier, inc=1, device_id={"inst": there, "tp": lax.rem(tp + shift, n_tp)},
+                        device_id_type=MESH_ID,
+                    )
+
     for copy in load_small:
         copy.wait()
     load_down.wait()
     load_up.wait()
+    for copy in load_hidden:
+        copy.start()
+    load_key.start()
     for k in range(n_act):
         row = lax.rem(pool_rows[me * n_act + k], pool_count)
         ranks = slice(k * rank, (k + 1) * rank)
@@ -85,7 +100,11 @@
         low_half[me, ranks, half:] = up[row]
         high_half[me, ranks, :] = down[row, :, half:]
 
-    pl.semaphore_wait(barrier, 2 + n_tp - 1)
+    pairs = 0
+    for _, end, helper, _ in ends:
+        for here in (end, helper):
+            pairs += jnp.where(me == here, 1, 0)
+    pl.semaphore_wait(barrier, 2 + (n_tp - 1) * (1 + pairs))
 
     right = {"inst": lax.rem(me + 1, n_inst)}
     left = {"inst": lax.rem(me + n_inst - 1, n_inst)}
@@ -115,9 +134,8 @@
     def arrive(h, owner):
         hop(h, owner, out_right_sem, right).wait_recv()
 
-    for h in range(2):
-        go_right(h, me)
-        go_left(h, me)
+    go_right(0, me)
+    go_left(0, me)
 
     for copy in load_hidden:
         copy.wait()
@@ -177,7 +195,17 @@
         cos_tab[s * requests : (s + 1) * requests, :] = jnp.cos(angle)
         sin_tab[s * requests : (s + 1) * requests, :] = jnp.where(lane < HEAD // 2, -sine, sine)
 
-    ends = ((0, 0, 1, right), (1, last, last - 1, left))
+    @pl.when(me < last)
+    def _():
+        hop(0, me, out_right_sem, right).wait_send()
+
+    go_right(1, me)
+
+    @pl.when(me > 0)
+    def _():
+        hop(0, me, out_left_sem, left).wait_send()
+
+    go_left(1, me)
 
     def send_guest(e, device):
         return (
@@ -190,7 +218,6 @@
 
         @pl.when(me == end)
         def _():
-            hop(0, me, sems, device).wait_send()
             if n_inst > 2:
                 hop(1, me, sems, device).wait_send()
             for copy in send_guest(e, device):
@@ -225,11 +252,13 @@
 
     lax.fori_loop(1, n_inst, step, 0)
 
-    def send_help(e, device):
-        return remote(help_out.at[e], help_in, help_out_sem.at[e], help_in_sem.at[e], device)
+    def send_help(e, shift):
+        return remote(
+            help_out.at[e], help_in.at[shift], help_out_sem.at[e, shift], help_in_sem.at[shift],
+            {"inst": ends[e][1], "tp": lax.rem(tp + shift, n_tp)},
+        )
 
     for e, end, helper, device in ends:
-        back = left if e == 0 else right
 
         @pl.when(me == helper)
         def _():
@@ -246,14 +275,8 @@
             help_out[e] = lax.fori_loop(
                 0, n_inst - 1, add_guest, jnp.zeros((rank, rows), jnp.float32)
             )
-            send_help(e, back).start()
-
-    for e, end, helper, device in ends:
-
-        @pl.when(me == end)
-        def _():
-            send_help(e, device).wait_recv()
-            score[...] += help_in[...]
+            for shift in range(n_tp):
+                send_help(e, shift).start()
 
     def send_score(shift):
         return remote(
@@ -268,11 +291,20 @@
         send_keys(shift).wait_recv()
         part[0] += keys_in[shift]
 
+    for shift in range(1, n_tp):
+        send_score(shift).wait_recv()
     shrink = score[...]
     for shift in range(1, n_tp):
-        send_score(shift).wait_recv()
         shrink += score_in[shift]
-    shrink = shrink.astype(jnp.bfloat16).astype(jnp.float32)
+    total_score[...] = shrink
+
+    @pl.when(is_end)
+    def _():
+        for shift in range(n_tp):
+            send_help(0, shift).wait_recv()
+            total_score[...] += help_in[shift]
+
+    shrink = total_score[...].astype(jnp.bfloat16).astype(jnp.float32)
 
     def add_update(owner, total):
         spread = jnp.concatenate(
@@ -304,17 +336,25 @@
 
         @pl.when(me == helper)
         def _():
-            send_help(e, device).wait_send()
+            for shift in range(n_tp):
+                send_help(e, shift).wait_send()
 
     def drain(owner, carry):
-        for h in range(2):
-            @pl.when((owner <= me) & (me + 1 < (last if h else n_inst)) & (me > 0))
-            def _():
-                hop(h, owner, out_right_sem, right).wait_send()
-
-            @pl.when((owner >= me) & (me > (1 if h else 0)) & (me < last))
-            def _():
-                hop(h, owner, out_left_sem, left).wait_send()
+        @pl.when((owner < me) & (me < last))
+        def _():
+            hop(0, owner, out_right_sem, right).wait_send()
+
+        @pl.when((owner > me) & (me > 0))
+        def _():
+            hop(0, owner, out_left_sem, left).wait_send()
+
+        @pl.when((owner <= me) & (me + 1 < last) & (me > 0))
+        def _():
+            hop(1, owner, out_right_sem, right).wait_send()
+
+        @pl.when((owner >= me) & (me > 1) & (me < last))
+        def _():
+            hop(1, owner, out_left_sem, left).wait_send()
 
         return carry
 
@@ -356,8 +396,9 @@
             pltpu.VMEM((n_tp, rows, local), jnp.float32),
             pltpu.VMEM((n_tp, rows, local), jnp.float32),
             pltpu.VMEM((rank, rows), jnp.float32),
+            pltpu.VMEM((rank, rows), jnp.float32),
             pltpu.VMEM((2, rank, rows), jnp.float32),
-            pltpu.VMEM((rank, rows), jnp.float32),
+            pltpu.VMEM((n_tp, rank, rows), jnp.float32),
             pltpu.VMEM((n_tp, rank, rows), jnp.float32),
             pltpu.VMEM((rows, HEAD), jnp.float32),
             pltpu.VMEM((rows, HEAD), jnp.float32),
@@ -368,15 +409,15 @@
             pltpu.SemaphoreType.DMA((2, n_inst)),
             pltpu.SemaphoreType.DMA((2, 2)),
             pltpu.SemaphoreType.DMA((2, 2)),
-            pltpu.SemaphoreType.DMA((2,)),
-            pltpu.SemaphoreType.DMA((2,)),
+            pltpu.SemaphoreType.DMA((2, n_tp)),
+            pltpu.SemaphoreType.DMA((n_tp,)),
             pltpu.SemaphoreType.DMA((n_tp,)),
             pltpu.SemaphoreType.DMA((n_tp,)),
             pltpu.SemaphoreType.DMA((n_tp,)),
             pltpu.SemaphoreType.DMA((n_tp,)),
         ],
         compiler_params=pltpu.CompilerParams(
-            collective_id=0, has_side_effects=True, vmem_limit_bytes=48 * 1024 * 1024
+            collective_id=0, has_side_effects=True, vmem_limit_bytes=60 * 1024 * 1024
         ),
         name="lora_keys",
     )(

time: 49.1 us -> 41.8 us (0.85)
  local copies, waits for them, and re-layouts: 7.73 us -> 1.57 us
  Pallas kernels: 41 us -> 40 us
    unnamed x15 -> x1, local copies, waits for them, and re-layouts: 7.73 us -> 1.57 us
    pallas_call x1, Pallas kernels: 41 us -> 40 us  [on_device(): pl.pallas_call(functools.partial(kernel, n_inst, n_tp, n_act, rank), out_...]
where the time goes in v3:
time: 41.8 us; the launch traced here: 41.6 us
  Pallas kernels  40 us (96%)
  local copies, waits for them, and re-layouts  1.57 us (4%)
    pallas_call x1, Pallas kernels, on_device(): pl.pallas_call(functools.partial(kernel, n_inst, n_tp, n_act, rank), out_...  40 us
    unnamed x1, local copies, waits for them, and re-layouts  1.57 us

profile of v3, /device:TPU:0, one launch (start us, length us, event | category | flops | bytes accessed | tf_op | source)
XLA Modules:
  0.0 41.6 jit_solution(8589198863240850967)
XLA Ops:
  0.0 40.0 %lora_keys.1 = bf16[2,128,256]{2,1,0:T(8,128)(2,1)} custom-call(s32[32]{0:T(128)} %pool_rows_hbm.1, s32[1,128]{1,0:T(1,128)} %bitcast.2, s32[1,128]{1,0:T(1,128)} %bitcast.3, f32[1,128]{1,0:T(1,128)} %constant.2.clone.freq_hbm, bf16[2,128,2048]{2,1,0:T(8,128)(2,1)} %hidden_hbm.1, bf16[2048,1024]{1,0:T(8,128)(2,1)} %key_hbm.1, ...), custom_call_target="tpu_custom_call" | custom-call | tf_op jit(solution)/shard_map/lora_keys/pallas_call | solution.py:378
  40.1 1.6 %copy.10 = bf16[2,128,256]{2,1,0:T(8,128)(2,1)} copy(bf16[2,128,256]{2,1,0:T(8,128)(2,1)} %lora_keys.1) | data formatting | bytes 262144

commit v4 on v3

--- a/solution.py
+++ b/solution.py
@@ -27,7 +27,7 @@
 def kernel(
     n_inst, n_tp, n_act, rank, pool_rows_hbm, slot_hbm, len_hbm, freq_hbm,
     hidden_hbm, key_hbm, down_hbm, up_hbm, out_ref,
-    pool_rows, slot, length, freq, hidden, key, down, up, low_half, high_half, guest, guest_slot,
+    pool_rows, slot, length, freq, hidden, key, down_low, down_high, up, low_half, high_half, guest, guest_slot,
     part, keys_in, score, total_score, help_out, help_in, score_in, cos_tab, sin_tab,
     small_sem, load_sem, out_right_sem, out_left_sem, in_sem, guest_out_sem, guest_in_sem,
     help_out_sem, help_in_sem, key_out_sem, key_in_sem, sc_out_sem, sc_in_sem,
@@ -37,11 +37,16 @@
     _, steps, requests, half = hidden.shape
     rows = steps * requests
     local = up.shape[2]
-    pool_count = down.shape[0]
+    pool_count = down_low.shape[0]
     last = n_inst - 1
     is_end = (me == 0) | (me == last)
 
-    load_down = pltpu.make_async_copy(down_hbm, down, load_sem.at[0])
+    load_down = [
+        pltpu.make_async_copy(
+            down_hbm.at[:, :, pl.ds(h * half, half)], down, load_sem.at[5 * h]
+        )
+        for h, down in enumerate((down_low, down_high))
+    ]
     load_up = pltpu.make_async_copy(up_hbm, up, load_sem.at[1])
     load_hidden = [
         pltpu.make_async_copy(
@@ -58,8 +63,9 @@
     ]
     for copy in load_small:
         copy.start()
-    load_down.start()
+    load_down[0].start()
     load_up.start()
+    load_down[1].start()
 
     barrier = pltpu.get_barrier_semaphore()
     for shift in (1, n_inst - 1):
@@ -88,17 +94,13 @@
 
     for copy in load_small:
         copy.wait()
-    load_down.wait()
+    own_rows = [lax.rem(pool_rows[me * n_act + k], pool_count) for k in range(n_act)]
+    load_down[0].wait()
     load_up.wait()
-    for copy in load_hidden:
-        copy.start()
-    load_key.start()
-    for k in range(n_act):
-        row = lax.rem(pool_rows[me * n_act + k], pool_count)
+    for k, row in enumerate(own_rows):
         ranks = slice(k * rank, (k + 1) * rank)
-        low_half[me, ranks, :half] = down[row, :, :half]
+        low_half[me, ranks, :half] = down_low[row]
         low_half[me, ranks, half:] = up[row]
-        high_half[me, ranks, :] = down[row, :, half:]
 
     pairs = 0
     for _, end, helper, _ in ends:
@@ -136,6 +138,13 @@
 
     go_right(0, me)
     go_left(0, me)
+
+    load_down[1].wait()
+    for copy in load_hidden:
+        copy.start()
+    load_key.start()
+    for k, row in enumerate(own_rows):
+        high_half[me, k * rank : (k + 1) * rank, :] = down_high[row]
 
     for copy in load_hidden:
         copy.wait()
@@ -223,6 +232,10 @@
             for copy in send_guest(e, device):
                 copy.start()
 
+    def add_guest(e, owner, total):
+        wanted = jnp.concatenate([guest_slot[e]] * steps, axis=1)
+        return pick(total, high_half[owner], guest[e].reshape(rows, half), wanted, owner)
+
     def step(d, carry):
         lower = me - d
         upper = me + d
@@ -236,18 +249,29 @@
 
         for owner, there, go_on in sides:
 
+            @pl.when(there)
+            def _():
+                add_low(owner)
+
+        for e, end, helper, device in ends:
+
+            @pl.when((me == helper) & (d == max(n_inst - 2, 1)))
+            def _():
+                for copy in send_guest(e, device):
+                    copy.wait_recv()
+                help_out[e] = lax.fori_loop(
+                    1, n_inst - 1, functools.partial(add_guest, e),
+                    jnp.zeros((rank, rows), jnp.float32),
+                )
+
+        for owner, there, go_on in sides:
+
             @pl.when(there & jnp.logical_not(is_end))
             def _():
                 arrive(1, owner)
                 go_on(1, owner)
                 add_high(owner)
 
-        for owner, there, go_on in sides:
-
-            @pl.when(there)
-            def _():
-                add_low(owner)
-
         return carry
 
     lax.fori_loop(1, n_inst, step, 0)
@@ -262,19 +286,7 @@
 
         @pl.when(me == helper)
         def _():
-            for copy in send_guest(e, device):
-                copy.wait_recv()
-            wanted = jnp.concatenate([guest_slot[e]] * steps, axis=1)
-
-            def add_guest(i, total):
-                owner = i + 1 - e
-                return pick(
-                    total, high_half[owner], guest[e].reshape(rows, half), wanted, owner
-                )
-
-            help_out[e] = lax.fori_loop(
-                0, n_inst - 1, add_guest, jnp.zeros((rank, rows), jnp.float32)
-            )
+            help_out[e] = add_guest(e, 0 if e else last, help_out[e])
             for shift in range(n_tp):
                 send_help(e, shift).start()
 
@@ -315,7 +327,7 @@
             (((0,), (0,)), ((), ())), preferred_element_type=jnp.float32,
         )
 
-    update = lax.fori_loop(0, n_inst, add_update, jnp.zeros((rows, local), jnp.float32))
+    update = lax.fori_loop(0, n_inst, add_update, jnp.zeros((rows, local), jnp.float32), unroll=n_inst <= 4)
     mixed = part[0] + ADAPTER_SCALE * update.astype(jnp.bfloat16).astype(jnp.float32)
     for h in range(local // HEAD):
         values = mixed[:, h * HEAD : (h + 1) * HEAD]
@@ -387,7 +399,8 @@
             pltpu.VMEM((1, HEAD), jnp.float32),
             pltpu.VMEM((2, steps, requests, half), jnp.bfloat16),
             pltpu.VMEM(key_matrix.shape, jnp.bfloat16),
-            pltpu.VMEM(down_weight.shape, jnp.bfloat16),
+            pltpu.VMEM((*down_weight.shape[:2], half), jnp.bfloat16),
+            pltpu.VMEM((*down_weight.shape[:2], half), jnp.bfloat16),
             pltpu.VMEM(up_weight.shape, jnp.bfloat16),
             pltpu.VMEM((n_inst, block, half + local), jnp.bfloat16),
             pltpu.VMEM((n_inst, block, half), jnp.bfloat16),
@@ -403,7 +416,7 @@
             pltpu.VMEM((rows, HEAD), jnp.float32),
             pltpu.VMEM((rows, HEAD), jnp.float32),
             pltpu.SemaphoreType.DMA((4,)),
-            pltpu.SemaphoreType.DMA((5,)),
+            pltpu.SemaphoreType.DMA((6,)),
             pltpu.SemaphoreType.DMA((2, n_inst)),
             pltpu.SemaphoreType.DMA((2, n_inst)),
             pltpu.SemaphoreType.DMA((2, n_inst)),

time: 41.8 us -> 41.5 us (level)
  no operation moved by 1% of the time
where the time goes in v4:
time: 41.5 us; the launch traced here: 41.3 us
  Pallas kernels  39.7 us (96%)
  local copies, waits for them, and re-layouts  1.57 us (4%)
    pallas_call x1, Pallas kernels, on_device(): pl.pallas_call(functools.partial(kernel, n_inst, n_tp, n_act, rank), out_...  39.7 us
    unnamed x1, local copies, waits for them, and re-layouts  1.57 us

profile of v4, /device:TPU:0, one launch (start us, length us, event | category | flops | bytes accessed | tf_op | source)
XLA Modules:
  0.0 41.3 jit_solution(13391767655111972435)
XLA Ops:
  0.0 39.7 %lora_keys.1 = bf16[2,128,256]{2,1,0:T(8,128)(2,1)} custom-call(s32[32]{0:T(128)} %pool_rows_hbm.1, s32[1,128]{1,0:T(1,128)} %bitcast.2, s32[1,128]{1,0:T(1,128)} %bitcast.3, f32[1,128]{1,0:T(1,128)} %constant.2.clone.freq_hbm, bf16[2,128,2048]{2,1,0:T(8,128)(2,1)} %hidden_hbm.1, bf16[2048,1024]{1,0:T(8,128)(2,1)} %key_hbm.1, ...), custom_call_target="tpu_custom_call" | custom-call | tf_op jit(solution)/shard_map/lora_keys/pallas_call | solution.py:390
  39.7 1.6 %copy.10 = bf16[2,128,256]{2,1,0:T(8,128)(2,1)} copy(bf16[2,128,256]{2,1,0:T(8,128)(2,1)} %lora_keys.1) | data formatting | bytes 262144

commit v5 on v4

--- a/solution.py
+++ b/solution.py
@@ -196,14 +196,6 @@
     add_low(me)
     add_high(me)
 
-    lens = jnp.broadcast_to(length[...].astype(jnp.float32), (HEAD, requests)).T
-    lane = lax.broadcasted_iota(jnp.int32, (requests, HEAD), 1)
-    for s in range(steps):
-        angle = (lens + float(s)) * freq[...]
-        sine = jnp.sin(angle)
-        cos_tab[s * requests : (s + 1) * requests, :] = jnp.cos(angle)
-        sin_tab[s * requests : (s + 1) * requests, :] = jnp.where(lane < HEAD // 2, -sine, sine)
-
     @pl.when(me < last)
     def _():
         hop(0, me, out_right_sem, right).wait_send()
@@ -235,6 +227,15 @@
     def add_guest(e, owner, total):
         wanted = jnp.concatenate([guest_slot[e]] * steps, axis=1)
         return pick(total, high_half[owner], guest[e].reshape(rows, half), wanted, owner)
+
+    def make_tables():
+        lens = jnp.broadcast_to(length[...].astype(jnp.float32), (HEAD, requests)).T
+        lane = lax.broadcasted_iota(jnp.int32, (requests, HEAD), 1)
+        for s in range(steps):
+            angle = (lens + float(s)) * freq[...]
+            sine = jnp.sin(angle)
+            cos_tab[s * requests : (s + 1) * requests, :] = jnp.cos(angle)
+            sin_tab[s * requests : (s + 1) * requests, :] = jnp.where(lane < HEAD // 2, -sine, sine)
 
     def step(d, carry):
         lower = me - d
@@ -252,6 +253,8 @@
             @pl.when(there)
             def _():
                 add_low(owner)
+
+        pl.when(d == 1)(make_tables)
 
         for e, end, helper, device in ends:
 

time: 41.5 us -> 41.5 us (level)
  no operation moved by 1% of the time
where the time goes in v5:
time: 41.5 us; the launch traced here: 41.3 us
  Pallas kernels  39.7 us (96%)
  local copies, waits for them, and re-layouts  1.57 us (4%)
    pallas_call x1, Pallas kernels, on_device(): pl.pallas_call(functools.partial(kernel, n_inst, n_tp, n_act, rank), out_...  39.7 us
    unnamed x1, local copies, waits for them, and re-layouts  1.57 us

profile of v5, /device:TPU:0, one launch (start us, length us, event | category | flops | bytes accessed | tf_op | source)
XLA Modules:
  0.0 41.3 jit_solution(10078033728251354684)
XLA Ops:
  0.0 39.7 %lora_keys.1 = bf16[2,128,256]{2,1,0:T(8,128)(2,1)} custom-call(s32[32]{0:T(128)} %pool_rows_hbm.1, s32[1,128]{1,0:T(1,128)} %bitcast.2, s32[1,128]{1,0:T(1,128)} %bitcast.3, f32[1,128]{1,0:T(1,128)} %constant.2.clone.freq_hbm, bf16[2,128,2048]{2,1,0:T(8,128)(2,1)} %hidden_hbm.1, bf16[2048,1024]{1,0:T(8,128)(2,1)} %key_hbm.1, ...), custom_call_target="tpu_custom_call" | custom-call | tf_op jit(solution)/shard_map/lora_keys/pallas_call | solution.py:393
  39.7 1.6 %copy.10 = bf16[2,128,256]{2,1,0:T(8,128)(2,1)} copy(bf16[2,128,256]{2,1,0:T(8,128)(2,1)} %lora_keys.1) | data formatting | bytes 262144

commit v6 on v5

--- a/solution.py
+++ b/solution.py
@@ -145,6 +145,8 @@
     load_key.start()
     for k, row in enumerate(own_rows):
         high_half[me, k * rank : (k + 1) * rank, :] = down_high[row]
+    go_right(1, me)
+    go_left(1, me)
 
     for copy in load_hidden:
         copy.wait()
@@ -195,18 +197,6 @@
     score[...] = jnp.zeros((rank, rows), jnp.float32)
     add_low(me)
     add_high(me)
-
-    @pl.when(me < last)
-    def _():
-        hop(0, me, out_right_sem, right).wait_send()
-
-    go_right(1, me)
-
-    @pl.when(me > 0)
-    def _():
-        hop(0, me, out_left_sem, left).wait_send()
-
-    go_left(1, me)
 
     def send_guest(e, device):
         return (
@@ -355,11 +345,11 @@
                 send_help(e, shift).wait_send()
 
     def drain(owner, carry):
-        @pl.when((owner < me) & (me < last))
+        @pl.when((owner <= me) & (me < last))
         def _():
             hop(0, owner, out_right_sem, right).wait_send()
 
-        @pl.when((owner > me) & (me > 0))
+        @pl.when((owner >= me) & (me > 0))
         def _():
             hop(0, owner, out_left_sem, left).wait_send()
 

time: 41.5 us -> 41.9 us (level)
  Pallas kernels: 39.7 us -> 40.2 us
    pallas_call x1, Pallas kernels: 39.7 us -> 40.2 us  [on_device(): pl.pallas_call(functools.partial(kernel, n_inst, n_tp, n_act, rank), out_...]
where the time goes in v6:
time: 41.9 us; the launch traced here: 41.8 us
  Pallas kernels  40.2 us (96%)
  local copies, waits for them, and re-layouts  1.57 us (4%)
    pallas_call x1, Pallas kernels, on_device(): pl.pallas_call(functools.partial(kernel, n_inst, n_tp, n_act, rank), out_...  40.2 us
    unnamed x1, local copies, waits for them, and re-layouts  1.57 us

profile of v6, /device:TPU:0, one launch (start us, length us, event | category | flops | bytes accessed | tf_op | source)
XLA Modules:
  0.0 41.8 jit_solution(10459902884515136933)
XLA Ops:
  0.0 40.2 %lora_keys.1 = bf16[2,128,256]{2,1,0:T(8,128)(2,1)} custom-call(s32[32]{0:T(128)} %pool_rows_hbm.1, s32[1,128]{1,0:T(1,128)} %bitcast.2, s32[1,128]{1,0:T(1,128)} %bitcast.3, f32[1,128]{1,0:T(1,128)} %constant.2.clone.freq_hbm, bf16[2,128,2048]{2,1,0:T(8,128)(2,1)} %hidden_hbm.1, bf16[2048,1024]{1,0:T(8,128)(2,1)} %key_hbm.1, ...), custom_call_target="tpu_custom_call" | custom-call | tf_op jit(solution)/shard_map/lora_keys/pallas_call | solution.py:383
  40.2 1.6 %copy.10 = bf16[2,128,256]{2,1,0:T(8,128)(2,1)} copy(bf16[2,128,256]{2,1,0:T(8,128)(2,1)} %lora_keys.1) | data formatting | bytes 262144

commit v7 on v4

--- a/solution.py
+++ b/solution.py
@@ -167,7 +167,6 @@
 
     for shift in range(1, n_tp):
         partial_keys(shift)
-        send_keys(shift).start()
     partial_keys(0)
 
     slots = jnp.concatenate([slot[...]] * steps, axis=1)
@@ -215,6 +214,9 @@
         hop(0, me, out_left_sem, left).wait_send()
 
     go_left(1, me)
+
+    for shift in range(1, n_tp):
+        send_keys(shift).start()
 
     def send_guest(e, device):
         return (

time: 41.5 us -> 41.5 us (level)
  no operation moved by 1% of the time
where the time goes in v7:
time: 41.5 us; the launch traced here: 41.3 us
  Pallas kernels  39.7 us (96%)
  local copies, waits for them, and re-layouts  1.57 us (4%)
    pallas_call x1, Pallas kernels, on_device(): pl.pallas_call(functools.partial(kernel, n_inst, n_tp, n_act, rank), out_...  39.7 us
    unnamed x1, local copies, waits for them, and re-layouts  1.57 us

profile of v7, /device:TPU:0, one launch (start us, length us, event | category | flops | bytes accessed | tf_op | source)
XLA Modules:
  0.0 41.3 jit_solution(3225746499463922927)
XLA Ops:
  0.0 39.7 %lora_keys.1 = bf16[2,128,256]{2,1,0:T(8,128)(2,1)} custom-call(s32[32]{0:T(128)} %pool_rows_hbm.1, s32[1,128]{1,0:T(1,128)} %bitcast.2, s32[1,128]{1,0:T(1,128)} %bitcast.3, f32[1,128]{1,0:T(1,128)} %constant.2.clone.freq_hbm, bf16[2,128,2048]{2,1,0:T(8,128)(2,1)} %hidden_hbm.1, bf16[2048,1024]{1,0:T(8,128)(2,1)} %key_hbm.1, ...), custom_call_target="tpu_custom_call" | custom-call | tf_op jit(solution)/shard_map/lora_keys/pallas_call | solution.py:392
  39.7 1.6 %copy.10 = bf16[2,128,256]{2,1,0:T(8,128)(2,1)} copy(bf16[2,128,256]{2,1,0:T(8,128)(2,1)} %lora_keys.1) | data formatting | bytes 262144
